TPU v7x, 256 devices: a whole 4x4x8 slice. The times are simulated.
256 devices in a mesh: grp: 128 (over x, y_hi, z, core), wide: 2 (over y_lo).
Axes of the slice: x: 4, y: 4 (y_hi: 2, y_lo: 2; y = y_hi * 2 + y_lo), z: 8, core: 2. Of those that a mesh axis runs over, the one named last changes fastest.
Arguments:
- ao_slab: bfloat16 [1024, 1200, 1200], P(('grp', 'wide')), may hold values from -6 to 6
- screen_mask: int32 [1024, 25, 25], P(('grp', 'wide')), may hold values 0 or 1
- pair_ao: int32 [1024, 2], P(('grp', 'wide')), may hold values from 0 to 1199
- occ_coef: bfloat16 [1200, 256], replicated, may hold values from -0.1875 to 0.1875
- vir_coef: bfloat16 [1200, 900], replicated, may hold values from -0.1875 to 0.1875
Outputs:
- mo_block: bfloat16 [256, 900, 1, 900], P(('grp', 'wide'))
All inputs are finite; a program needn't handle non-finite values. No bound on the sum of `screen_mask` on one device may be relied on, other than what follows from the above.
Results may differ from a plain program's by a relative error of at most 0.007.
Values may be sent and summed in bfloat16 or wider, within the bound.
A program may use at most 128 MiB of HBM per device.

v0:
```python
import jax
import jax.numpy as jnp
from jax import lax
from jax.sharding import PartitionSpec as P

NBF = 1200
JWIN = 1


def shards(ao_slab, screen_mask, pair_ao, occ_coef, vir_coef):
    pairs_here, nbf_local, _ = ao_slab.shape
    block_count = screen_mask.shape[1]
    block_size = nbf_local // block_count
    n_group = lax.axis_size("grp")
    n_slabs = lax.axis_size("wide")
    nvir_all = vir_coef.shape[1]

    def half_transform(pair_slot):
        screened = (
            ao_slab[pair_slot].reshape(block_count, block_size, block_count, block_size)
            * screen_mask[pair_slot][:, None, :, None].astype(jnp.bfloat16)
        ).reshape(nbf_local, nbf_local)
        left = lax.dot_general(
            occ_coef, screened, (((0,), (0,)), ((), ())), preferred_element_type=jnp.float32
        ).astype(jnp.bfloat16)
        return jnp.dot(left, vir_coef, preferred_element_type=jnp.float32).astype(jnp.bfloat16)

    halves = jnp.stack([half_transform(pair_slot) for pair_slot in range(pairs_here)])
    every_pair = lax.all_gather(pair_ao, ("grp", "wide"), axis=0, tiled=True)
    total_pairs = every_pair.shape[0]
    regrouped = lax.all_to_all(
        lax.all_to_all(halves, "grp", split_axis=1, concat_axis=0, tiled=True),
        "wide",
        split_axis=1,
        concat_axis=0,
        tiled=True,
    )
    pair_rows = (
        every_pair.reshape(n_group, n_slabs, pairs_here, 2)
        .transpose(1, 0, 2, 3)
        .reshape(total_pairs, 2)
    )
    lambda_rows = occ_coef[pair_rows[:, 0], :JWIN].astype(jnp.float32)
    sigma_rows = vir_coef[pair_rows[:, 1]].astype(jnp.float32)
    pair_kernel = (lambda_rows[:, :, None] * sigma_rows[:, None, :]).astype(jnp.bfloat16)
    pair_kernel = pair_kernel.reshape(total_pairs, JWIN * nvir_all)
    summed = lax.dot_general(
        regrouped, pair_kernel, (((0,), (0,)), ((), ())), preferred_element_type=jnp.float32
    )
    scaled = summed * (NBF / total_pairs**0.5)
    local_occ = regrouped.shape[1]
    return scaled.astype(jnp.bfloat16).reshape(local_occ, nvir_all, JWIN, nvir_all)


def solution(mesh):
    in_specs = (
        P(("grp", "wide"), None, None),
        P(("grp", "wide"), None, None),
        P(("grp", "wide"), None),
        P(),
        P(),
    )
    out_specs = P(("grp", "wide"), None, None, None)
    return jax.shard_map(shards, mesh=mesh, in_specs=in_specs, out_specs=out_specs, check_vma=False)
```

profile of v0, /device:TPU:1, one launch (start us, length us, event | category | flops | bytes accessed | tf_op | source)
XLA Modules:
  0.0 840.1 jit_solution(13561897833054850711)
XLA Ops:
  0.0 0.0 copy-start
  0.0 0.9 copy_convert_fusion
  0.9 5.0 mul.75
  5.9 13.8 %mul.76 = bf16[1200,1200]{1,0:T(8,128)(2,1)} reshape(bf16[25,48,25,48]{3,2,1,0:T(8,128)(2,1)} %mul.75) | data formatting | bytes 5760000 | tf_op jit(solution)/shard_map/mul | solution.py:20
  19.7 5.1 mul.78
  24.7 13.9 %mul.79 = bf16[1200,1200]{1,0:T(8,128)(2,1)} reshape(bf16[25,48,25,48]{3,2,1,0:T(8,128)(2,1)} %mul.78) | data formatting | bytes 5760000 | tf_op jit(solution)/shard_map/mul | solution.py:20
  38.6 0.0 copy-done
  38.6 5.6 fusion.21
  44.3 6.4 fusion.22
  50.7 5.1 mul.81
  55.8 13.8 %mul.82 = bf16[1200,1200]{1,0:T(8,128)(2,1)} reshape(bf16[25,48,25,48]{3,2,1,0:T(8,128)(2,1)} %mul.81) | data formatting | bytes 5760000 | tf_op jit(solution)/shard_map/mul | solution.py:20
  69.6 6.4 fusion.23
  76.0 5.1 mul.84
  81.1 13.8 %mul.85 = bf16[1200,1200]{1,0:T(8,128)(2,1)} reshape(bf16[25,48,25,48]{3,2,1,0:T(8,128)(2,1)} %mul.84) | data formatting | bytes 5760000 | tf_op jit(solution)/shard_map/mul | solution.py:20
  94.9 6.4 fusion.24
  101.3 2.8 pad_maximum_fusion
  104.0 3.3 copy.14
  107.4 68.5 %all_to_all.33 = bf16[4,256,900]{2,0,1:T(4,128)(2,1)S(1)} all-to-all(bf16[4,256,900]{2,0,1:T(4,128)(2,1)S(1)} %copy.14), channel_id=1, replica_groups=mesh['grp'=128,'wide'=2] {'grp'}, dimensions={1} | all-to-all | bytes 3686400 | tf_op jit(solution)/shard_map/all_to_all | solution.py:32
  175.9 2.4 copy.15
  178.3 4.5 copy.16
  182.8 4.7 all-to-all-start.1
  187.5 0.0 copy-start.3
  187.6 3.2 copy.19
  190.7 626.4 %all-gather = s32[256,4,2]{1,2,0:T(2,128)S(1)} all-gather(s32[1,4,2]{1,2,0:T(2,128)S(1)} %bitcast.103), channel_id=1, replica_groups=mesh['grp'=128,'wide'=2] {'grp','wide'}, dimensions={0}, use_global_device_ids=true | all-gather | bytes 8224 | tf_op jit(solution)/shard_map/all_gather | solution.py:29
  817.1 0.2 reshape.118
  817.3 9.2 %gather_fusion = bf16[1024]{0:T(1024)(128)(2,1)S(1)} fusion(bf16[1200,256]{1,0:T(8,128)(2,1)S(1)} %copy-done, s32[1024]{0:T(1024)S(1)} %bitcast.94), kind=kCustom, calls=%fused_computation | custom fusion | bytes 12288 | tf_op jit(solution)/shard_map/gather | solution.py:43
  826.5 5.3 gather_fusion.1
  831.8 0.0 all-to-all-done.1
  831.8 2.9 copy.24
  834.8 1.4 pad.6
  836.2 0.5 copy.20
  836.7 3.4 fusion.18
  (10 shorter events, 0.1 us)
Async XLA Ops:
  0.0 38.6 %copy-start = (bf16[1200,256]{1,0:T(8,128)(2,1)S(1)}, bf16[1200,256]{1,0:T(8,128)(2,1)}, u32[]{:S(2)}) copy-start(bf16[1200,256]{1,0:T(8,128)(2,1)} %param.8) | copy-start | bytes 1843204
  24.7 13.9 %copy-start.1 = (bf16[1200,900]{0,1:T(8,128)(2,1)S(1)}, bf16[1200,900]{0,1:T(8,128)(2,1)}, u32[]{:S(2)}) copy-start(bf16[1200,900]{0,1:T(8,128)(2,1)} %param.9) | copy-start | bytes 6480004
  182.8 649.0 %all-to-all-start.1 = ((bf16[512,2,900]{0,2,1:T(8,128)(2,1)}), bf16[512,2,900]{0,2,1:T(8,128)(2,1)}, u32[]{:S(2)}, u32[]{:S(2)}) async-start(bf16[512,2,900]{0,2,1:T(8,128)(2,1)} %copy.16), calls=%async_computation.1 | async-start | bytes 3702784 | tf_op jit(solution)/shard_map/all_to_all | solution.py:31
  187.5 3.2 copy-start.3
  834.8 1.9 copy-start.2
where the time goes:
time: 845 us; the launch traced here: 840 us
  blocking collectives  695 us (82%)
  local copies, waits for them, and re-layouts  108 us (13%)
  matrix products  28.3 us (3%)
    all_gather x1, blocking collectives, shards(): every_pair = lax.all_gather(pair_ao, ('grp', 'wide'), axis=0, tiled=True)  626 us
    mul x8, local copies, waits for them, and re-layouts, half_transform(): ao_slab[pair_slot].reshape(block_count, block_size, block_count, block_size)  75.5 us
    all_to_all x1, blocking collectives, shards(): lax.all_to_all(halves, 'grp', split_axis=1, concat_axis=0, tiled=True)  68.5 us
    dot_general x4, matrix products, half_transform(): jnp.dot(left, vir_coef, preferred_element_type=jnp.float32)  24.9 us
  transfers between devices with their start and end apart: 1, of which 0 were waited for; matrix products, arithmetic and copies ran while one was open for 2% of the time, Pallas kernels for 0%

commit v1 on v0

v1 whole, which is shorter than its diff:
```python
import jax
import jax.numpy as jnp
from jax import lax
from jax.experimental import pallas as pl
from jax.experimental.pallas import tpu as pltpu
from jax.sharding import PartitionSpec as P

MESH = pl.DeviceIdType.MESH
BF16 = jnp.bfloat16
F32 = jnp.float32

NBF = 1200
NBP = 1280
NOCC = 256
NVIR = 900
NVP = 1024
NBLK = 25
BLK = NBF // NBLK
PAIRS_HERE = 4
SIDE = 16
PAIRS = 1024
SCALE = NBF / PAIRS**0.5
NN = (((1,), (0,)), ((), ()))
NT = (((1,), (1,)), ((), ()))
TN = (((0,), (0,)), ((), ()))


def dot(a, b, dims):
    return lax.dot_general(a, b, dims, preferred_element_type=F32)


def iota(shape, axis):
    return lax.broadcasted_iota(jnp.int32, shape, axis)


def one_hot(hit):
    return jnp.where(hit, 1.0, 0.0).astype(BF16)


def kernel(
    ao, mask_ref, pair_ref, occ, vir, out,
    aob, occb, virb, virt, occt, perm, mx, scr, left, half, recv, turned, final, pk, acc, outb,
    idx_own, idx_z, idx_zrow, idx_all,
    ao_sem, in_sem, out_sem, send1, recv1, send2, recv2, idx_send, idx_recv,
):
    grp = lax.axis_index("grp")
    wide = lax.axis_index("wide")
    zc = lax.rem(grp, SIDE)
    xy = lax.div(grp, SIDE) * 2 + wide

    def at(xy_of, zc_of):
        return (lax.div(xy_of, 2) * SIDE + zc_of, lax.rem(xy_of, 2))

    occ_copy = pltpu.make_async_copy(occ, occb.at[0:NBF], in_sem.at[0])
    vir_copy = pltpu.make_async_copy(vir, virb, in_sem.at[1])
    ao_copies = [pltpu.make_async_copy(ao.at[p], aob.at[p], ao_sem.at[p]) for p in range(PAIRS_HERE)]
    occ_copy.start()
    ao_copies[0].start()
    vir_copy.start()
    for p in range(1, PAIRS_HERE):
        ao_copies[p].start()

    barrier = pltpu.get_barrier_semaphore()

    def greet(k, carry):
        pl.semaphore_signal(
            barrier, inc=1, device_id=at(xy, lax.rem(zc + k, SIDE)), device_id_type=MESH
        )
        pl.semaphore_signal(
            barrier, inc=1, device_id=at(lax.rem(xy + k, SIDE), zc), device_id_type=MESH
        )
        return carry

    lax.fori_loop(1, SIDE, greet, 0)

    row = iota((NOCC, NOCC), 0)
    col = iota((NOCC, NOCC), 1)
    hi = lax.shift_right_logical(row, 4)
    lo = row & 15

    def owner(xy_of, zc_of):
        return (lax.shift_right_logical(xy_of, 1) * SIDE + zc_of) * 2 + (xy_of & 1)

    perm[0] = one_hot(col == owner(lo, hi))
    perm[1] = one_hot(col == owner(hi, lo))
    perm[2] = one_hot(col == row)
    perm[3] = one_hot(col == lo * SIDE + hi)

    block_of = iota((NBLK, NBP), 0) * BLK
    lane = iota((NBLK, NBP), 1)
    spread = one_hot((lane >= block_of) & (lane < block_of + BLK))
    for p in range(PAIRS_HERE):
        mx[p, 0:NBLK] = dot(mask_ref[:, p, :].astype(F32).astype(BF16), spread, NN)

    lane8 = iota((8, 128), 1)
    own = jnp.zeros((8, 128), jnp.int32)
    for p in range(PAIRS_HERE):
        for q in range(2):
            own = jnp.where(lane8 == 2 * p + q, pair_ref[q : q + 1, p : p + 1], own)
    idx_own[...] = own
    idx_z[zc] = own

    scr[NBF:NBP, :] = jnp.zeros((NBP - NBF, NBP), BF16)
    scr[0:NBF, NBP - 128 : NBP] = jnp.zeros((NBF, 128), BF16)
    occb[NBF:NBP, :] = jnp.zeros((NBP - NBF, NOCC), BF16)
    virt[:, NBP - 128 : NBP] = jnp.zeros((NVP, 128), BF16)
    virt[NVIR - 4 : NVP, :] = jnp.zeros((NVP - NVIR + 4, NBP), BF16)

    occ_copy.wait()
    for q in range(2):
        occt[q] = dot(perm[q], occb[...], NT).astype(BF16)

    def phase1(p, carry):
        q = lax.rem(p, 2)
        pltpu.make_async_copy(ao.at[0], aob.at[p], ao_sem.at[p]).wait()

        def screen(r, c):
            rows = pl.ds(pl.multiple_of(r * BLK, BLK), BLK)
            keep = mx[p, pl.ds(r, 1), 0:NBF].astype(BF16)
            scr[rows, 0:NBF] = aob[p, rows, :] * keep
            return c

        lax.fori_loop(0, NBLK, screen, 0)
        left[...] = dot(occt[q], scr[...], NN).astype(BF16)

        @pl.when(p == 0)
        def _():
            vir_copy.wait()
            virt[0:NVIR, 0:NBF] = virb[...]

        half[p] = dot(left[...], virt[...], NT).astype(BF16)

        @pl.when(p == 0)
        def _():
            pl.semaphore_wait(barrier, 2 * (SIDE - 1))

            def share(k, c):
                pltpu.make_async_remote_copy(
                    src_ref=idx_own, dst_ref=idx_z.at[zc],
                    send_sem=idx_send.at[0], recv_sem=idx_recv.at[0],
                    device_id=at(xy, lax.rem(zc + k, SIDE)), device_id_type=MESH,
                ).start()
                return c

            lax.fori_loop(1, SIDE, share, 0)

        me = zc + q * (xy - zc)

        def send(k, c):
            to = lax.rem(me + k, SIDE)
            pltpu.make_async_remote_copy(
                src_ref=half.at[p, pl.ds(pl.multiple_of(to * SIDE, SIDE), SIDE)],
                dst_ref=recv.at[p, pl.ds(pl.multiple_of(me * SIDE, SIDE), SIDE)],
                send_sem=send1.at[p], recv_sem=recv1.at[p],
                device_id=at(xy + q * (to - xy), to + q * (zc - to)), device_id_type=MESH,
            ).start()
            return c

        lax.fori_loop(1, SIDE, send, 0)
        mine = pl.ds(pl.multiple_of(me * SIDE, SIDE), SIDE)
        recv[p, mine] = half[p, mine]
        return carry

    lax.fori_loop(0, PAIRS_HERE, phase1, 0)

    def got(ref, sem):
        pltpu.make_async_copy(ref, ref, sem).wait()

    got(idx_z.at[0 : SIDE - 1], idx_recv.at[0])
    idx_zrow[...] = idx_z[:, 0, :]
    idx_all[xy] = idx_z[:, 0, :]

    def share2(k, c):
        pltpu.make_async_remote_copy(
            src_ref=idx_zrow, dst_ref=idx_all.at[xy],
            send_sem=idx_send.at[1], recv_sem=idx_recv.at[1],
            device_id=at(lax.rem(xy + k, SIDE), zc), device_id_type=MESH,
        ).start()
        return c

    lax.fori_loop(1, SIDE, share2, 0)
    got(idx_all.at[0 : SIDE - 1], idx_recv.at[1])

    lane_all = iota((NOCC, 128), 1)
    basis = iota((NOCC, NBP), 1)

    def build(p, c):
        table = idx_all[...].reshape(NOCC, 128).astype(F32)

        def chosen(j):
            return jnp.sum(jnp.where(lane_all == j, table, 0.0), axis=1, keepdims=True).astype(jnp.int32)

        lam = dot(one_hot(basis == chosen(2 * p)), occb[:, 0:128], NN)[:, 0:1]
        rows = dot(one_hot(basis == chosen(2 * p + 1)), virt[...], NT)
        kernel_rows = (lam * rows).astype(BF16)
        pk[p] = dot(perm[2 + lax.rem(p, 2)], kernel_rows, NN).astype(BF16)
        return c

    lax.fori_loop(0, PAIRS_HERE, build, 0)

    def phase2(p):
        q = p % 2
        got(recv.at[p, 0 : (SIDE - 1) * SIDE], recv1.at[p])
        turned[p] = dot(perm[3], recv[p], NN).astype(BF16)
        me = xy if q == 0 else zc

        def send(k, c):
            to = lax.rem(me + k, SIDE)
            pltpu.make_async_remote_copy(
                src_ref=turned.at[p, pl.ds(pl.multiple_of(to * SIDE, SIDE), SIDE)],
                dst_ref=final.at[p, pl.ds(pl.multiple_of(me * SIDE, SIDE), SIDE)],
                send_sem=send2.at[p], recv_sem=recv2.at[p],
                device_id=at(to, zc) if q == 0 else at(xy, to), device_id_type=MESH,
            ).start()
            return c

        lax.fori_loop(1, SIDE, send, 0)
        mine = pl.ds(pl.multiple_of(me * SIDE, SIDE), SIDE)
        final[p, mine] = turned[p, mine]

    def add(p, first=False, last=False):
        got(final.at[p, 0 : (SIDE - 1) * SIDE], recv2.at[p])
        for a0 in range(0, NVP, 256):
            rows = pl.ds(a0, 256)
            term = dot(final[p, :, rows], pk[p], TN)
            if not first:
                term = acc[rows] + term
            if last:
                n = min(256, NVIR - a0)
                outb[a0 : a0 + n] = (term[0:n, 0:NVIR] * SCALE).astype(BF16)
                pltpu.make_async_copy(outb.at[a0 : a0 + n], out.at[a0 : a0 + n], out_sem.at[a0 // 256]).start()
            else:
                acc[rows] = term

    phase2(0)
    phase2(1)
    phase2(2)
    add(0, first=True)
    phase2(3)
    add(2)
    add(1)
    add(3, last=True)

    for p in range(PAIRS_HERE):
        got(half.at[p, 0 : (SIDE - 1) * SIDE], send1.at[p])
        got(turned.at[p, 0 : (SIDE - 1) * SIDE], send2.at[p])
    got(idx_z.at[0 : SIDE - 1], idx_send.at[0])
    got(idx_all.at[0 : SIDE - 1], idx_send.at[1])
    for a0 in range(0, NVP, 256):
        n = min(256, NVIR - a0)
        pltpu.make_async_copy(outb.at[a0 : a0 + n], out.at[a0 : a0 + n], out_sem.at[a0 // 256]).wait()


def shards(ao_slab, screen_mask, pair_ao, occ_coef, vir_coef):
    any_space = pl.BlockSpec(memory_space=pl.ANY)
    vmem = pl.BlockSpec(memory_space=pltpu.VMEM)
    dma = pltpu.SemaphoreType.DMA
    block = pl.pallas_call(
        kernel,
        name="mo_block",
        out_shape=jax.ShapeDtypeStruct((NVIR, NVIR), BF16),
        in_specs=[any_space, vmem, vmem, any_space, any_space],
        out_specs=any_space,
        scratch_shapes=[
            pltpu.VMEM((PAIRS_HERE, NBF, NBF), BF16),
            pltpu.VMEM((NBP, NOCC), BF16),
            pltpu.VMEM((NVIR, NBF), BF16),
            pltpu.VMEM((NVP, NBP), BF16),
            pltpu.VMEM((2, NOCC, NBP), BF16),
            pltpu.VMEM((4, NOCC, NOCC), BF16),
            pltpu.VMEM((PAIRS_HERE, 32, NBP), F32),
            pltpu.VMEM((NBP, NBP), BF16),
            pltpu.VMEM((NOCC, NBP), BF16),
            pltpu.VMEM((PAIRS_HERE, NOCC, NVP), BF16),
            pltpu.VMEM((PAIRS_HERE, NOCC, NVP), BF16),
            pltpu.VMEM((PAIRS_HERE, NOCC, NVP), BF16),
            pltpu.VMEM((PAIRS_HERE, NOCC, NVP), BF16),
            pltpu.VMEM((PAIRS_HERE, NOCC, NVP), BF16),
            pltpu.VMEM((NVP, NVP), F32),
            pltpu.VMEM((NVIR, NVIR), BF16),
            pltpu.VMEM((8, 128), jnp.int32),
            pltpu.VMEM((SIDE, 8, 128), jnp.int32),
            pltpu.VMEM((SIDE, 128), jnp.int32),
            pltpu.VMEM((SIDE, SIDE, 128), jnp.int32),
            dma((PAIRS_HERE,)),
            dma((2,)),
            dma((4,)),
            dma((PAIRS_HERE,)),
            dma((PAIRS_HERE,)),
            dma((PAIRS_HERE,)),
            dma((PAIRS_HERE,)),
            dma((2,)),
            dma((2,)),
        ],
        compiler_params=pltpu.CompilerParams(
            collective_id=0, has_side_effects=True, vmem_limit_bytes=56 << 20
        ),
        cost_estimate=pl.CostEstimate(flops=7_000_000_000, bytes_accessed=16_000_000, transcendentals=0),
    )(ao_slab, screen_mask.transpose(1, 0, 2), pair_ao.T, occ_coef, vir_coef.T)
    return block.reshape(1, NVIR, 1, NVIR)


def solution(mesh):
    in_specs = (
        P(("grp", "wide"), None, None),
        P(("grp", "wide"), None, None),
        P(("grp", "wide"), None),
        P(),
        P(),
    )
    out_specs = P(("grp", "wide"), None, None, None)
    return jax.shard_map(shards, mesh=mesh, in_specs=in_specs, out_specs=out_specs, check_vma=False)
```

time: 845 us -> 70.3 us (0.08)
  blocking collectives: 695 us -> 0 us
  local copies, waits for them, and re-layouts: 108 us -> 2.89 us
  Pallas kernels: 0 us -> 67.3 us
  matrix products: 28.3 us -> 0 us
    all_gather x1 -> x0, blocking collectives: 626 us -> none  [shards(): every_pair = lax.all_gather(pair_ao, ('grp', 'wide'), axis=0, tiled=True)]
    mul x8 -> x0, local copies, waits for them, and re-layouts: 75.5 us -> none  [half_transform(): ao_slab[pair_slot].reshape(block_count, block_size, block_count, block_size)]
    all_to_all x1 -> x0, blocking collectives: 68.5 us -> none  [shards(): lax.all_to_all(halves, 'grp', split_axis=1, concat_axis=0, tiled=True)]
    pallas_call x0 -> x1, Pallas kernels: none -> 67.3 us  [shards(): pl.pallas_call(kernel, name='mo_block', out_shape=jax.ShapeDtypeStruct((N...]
    dot_general x5 -> x0, matrix products: 28.3 us -> none  [the longest x4 24.9 us: half_transform(): jnp.dot(left, vir_coef, preferred_element_type=jnp.float32)]
    gather x2 -> x0, local copies, waits for them, and re-layouts: 14.5 us -> none  [the longest x1 9.17 us: shards(): lambda_rows = occ_coef[pair_rows[:, 0], :JWIN].astype(jnp.float32)]
    all_to_all x3 -> x0, local copies, waits for them, and re-layouts: 9.81 us -> none  [the longest x2 6.89 us: shards(): lax.all_to_all(halves, 'grp', split_axis=1, concat_axis=0, tiled=True)]
  transfers between devices with their start and end apart: 1 -> 0, of which waited for: 0 -> 0; matrix products, arithmetic and copies ran while one was open for 2% -> 0% of each run, Pallas kernels for 0% -> 0%
where the time goes in v1:
time: 70.3 us; the launch traced here: 70.2 us
  Pallas kernels  67.3 us (96%)
  local copies, waits for them, and re-layouts  2.89 us (4%)
    pallas_call x1, Pallas kernels, shards(): pl.pallas_call(kernel, name='mo_block', out_shape=jax.ShapeDtypeStruct((N...  67.3 us
    unnamed x1, local copies, waits for them, and re-layouts  2.89 us

profile of v1, /device:TPU:1, one launch (start us, length us, event | category | flops | bytes accessed | tf_op | source)
XLA Modules:
  0.0 70.2 jit_solution(527021980109322249)
XLA Ops:
  0.0 67.3 %mo_block.1 = bf16[900,900]{1,0:T(8,128)(2,1)} custom-call(bf16[4,1200,1200]{2,1,0:T(8,128)(2,1)} %ao.1, s32[25,4,25]{2,1,0:T(4,128)} %bitcast.6, s32[2,4]{1,0:T(2,128)} %bitcast.7, bf16[1200,256]{1,0:T(8,128)(2,1)} %occ.1, bf16[900,1200]{1,0:T(8,128)(2,1)} %bitcast.5), custom_call_target="tpu_custom_call" | custom-call | flops 7000000000 | bytes 16000000 | tf_op jit(solution)/shard_map/mo_block/pallas_call | solution.py:258
  67.3 2.9 %copy.7 = bf16[1,900,1,900]{3,1,2,0:T(8,128)(2,1)} copy(bf16[1,900,1,900]{3,1,2,0:T(8,128)(2,1)} %bitcast.4) | data formatting | bytes 3240000

commit v2 on v1

--- a/solution.py
+++ b/solution.py
@@ -14,6 +14,8 @@
 NOCC = 256
 NVIR = 900
 NVP = 1024
+WIDE = 896
+REST = NVIR - WIDE
 NBLK = 25
 BLK = NBF // NBLK
 PAIRS_HERE = 4
@@ -38,10 +40,11 @@
 
 
 def kernel(
-    ao, mask_ref, pair_ref, occ, vir, out,
-    aob, occb, virb, virt, occt, perm, mx, scr, left, half, recv, turned, final, pk, acc, outb,
+    ao, mask, pair, occ, vir, out,
+    mask_ref, pair_ref, aob, occb, virb, virt, occt, perm, mx, scr, left, half, recv, turned, final,
+    rest, rest_own, rest_recv, rest_turned, rest_final, pk, pkt, acc,
     idx_own, idx_z, idx_zrow, idx_all,
-    ao_sem, in_sem, out_sem, send1, recv1, send2, recv2, idx_send, idx_recv,
+    ao_sem, in_sem, send1, recv1, send2, recv2, rest_send, rest_sem, idx_send, idx_recv,
 ):
     grp = lax.axis_index("grp")
     wide = lax.axis_index("wide")
@@ -54,6 +57,10 @@
     occ_copy = pltpu.make_async_copy(occ, occb.at[0:NBF], in_sem.at[0])
     vir_copy = pltpu.make_async_copy(vir, virb, in_sem.at[1])
     ao_copies = [pltpu.make_async_copy(ao.at[p], aob.at[p], ao_sem.at[p]) for p in range(PAIRS_HERE)]
+    mask_copy = pltpu.make_async_copy(mask, mask_ref, in_sem.at[2])
+    pair_copy = pltpu.make_async_copy(pair, pair_ref, in_sem.at[3])
+    mask_copy.start()
+    pair_copy.start()
     occ_copy.start()
     ao_copies[0].start()
     vir_copy.start()
@@ -89,11 +96,13 @@
     block_of = iota((NBLK, NBP), 0) * BLK
     lane = iota((NBLK, NBP), 1)
     spread = one_hot((lane >= block_of) & (lane < block_of + BLK))
+    mask_copy.wait()
     for p in range(PAIRS_HERE):
         mx[p, 0:NBLK] = dot(mask_ref[:, p, :].astype(F32).astype(BF16), spread, NN)
 
     lane8 = iota((8, 128), 1)
     own = jnp.zeros((8, 128), jnp.int32)
+    pair_copy.wait()
     for p in range(PAIRS_HERE):
         for q in range(2):
             own = jnp.where(lane8 == 2 * p + q, pair_ref[q : q + 1, p : p + 1], own)
@@ -128,7 +137,9 @@
             vir_copy.wait()
             virt[0:NVIR, 0:NBF] = virb[...]
 
-        half[p] = dot(left[...], virt[...], NT).astype(BF16)
+        both = dot(left[...], virt[...], NT)
+        half[p] = both[:, 0:WIDE].astype(BF16)
+        rest[p] = both[:, WIDE:NVP].astype(BF16)
 
         @pl.when(p == 0)
         def _():
@@ -166,6 +177,38 @@
     def got(ref, sem):
         pltpu.make_async_copy(ref, ref, sem).wait()
 
+    def slab(ref, k):
+        return ref.at[pl.ds(pl.multiple_of(k * SIDE, SIDE), SIDE)]
+
+    def spread_out(src, dst, me, to_device, sends, recvs):
+        def send(k, c):
+            to = lax.rem(me + k, SIDE)
+            pltpu.make_async_remote_copy(
+                src_ref=slab(src, to), dst_ref=slab(dst, me), send_sem=sends, recv_sem=recvs,
+                device_id=to_device(to), device_id_type=MESH,
+            ).start()
+            return c
+
+        lax.fori_loop(1, SIDE, send, 0)
+        slab(dst, me)[...] = slab(src, me)[...]
+
+    def along_z(to):
+        return at(xy, to)
+
+    def along_xy(to):
+        return at(to, zc)
+
+    shift_row = iota((128, 128), 0)
+    shift_col = iota((128, 128), 1)
+    total = jnp.zeros((NOCC, 128), F32)
+    for p in range(PAIRS_HERE):
+        moved = dot(rest[p], one_hot((shift_col == shift_row + REST * p) & (shift_row < REST)), NN)
+        if p % 2:
+            moved = dot(perm[3], moved.astype(BF16), NN)
+        total = total + moved
+    rest_own[...] = total.astype(BF16)
+    spread_out(rest_own, rest_recv, zc, along_z, rest_send.at[0], rest_sem.at[0])
+
     got(idx_z.at[0 : SIDE - 1], idx_recv.at[0])
     idx_zrow[...] = idx_z[:, 0, :]
     idx_all[xy] = idx_z[:, 0, :]
@@ -193,7 +236,8 @@
         lam = dot(one_hot(basis == chosen(2 * p)), occb[:, 0:128], NN)[:, 0:1]
         rows = dot(one_hot(basis == chosen(2 * p + 1)), virt[...], NT)
         kernel_rows = (lam * rows).astype(BF16)
-        pk[p] = dot(perm[2 + lax.rem(p, 2)], kernel_rows, NN).astype(BF16)
+        pk[p] = kernel_rows
+        pkt[p] = dot(perm[2 + lax.rem(p, 2)], kernel_rows, NN).astype(BF16)
         return c
 
     lax.fori_loop(0, PAIRS_HERE, build, 0)
@@ -202,41 +246,43 @@
         q = p % 2
         got(recv.at[p, 0 : (SIDE - 1) * SIDE], recv1.at[p])
         turned[p] = dot(perm[3], recv[p], NN).astype(BF16)
-        me = xy if q == 0 else zc
-
-        def send(k, c):
-            to = lax.rem(me + k, SIDE)
-            pltpu.make_async_remote_copy(
-                src_ref=turned.at[p, pl.ds(pl.multiple_of(to * SIDE, SIDE), SIDE)],
-                dst_ref=final.at[p, pl.ds(pl.multiple_of(me * SIDE, SIDE), SIDE)],
-                send_sem=send2.at[p], recv_sem=recv2.at[p],
-                device_id=at(to, zc) if q == 0 else at(xy, to), device_id_type=MESH,
-            ).start()
-            return c
-
-        lax.fori_loop(1, SIDE, send, 0)
-        mine = pl.ds(pl.multiple_of(me * SIDE, SIDE), SIDE)
-        final[p, mine] = turned[p, mine]
+        if q == 0:
+            spread_out(turned.at[p], final.at[p], xy, along_xy, send2.at[p], recv2.at[p])
+        else:
+            spread_out(turned.at[p], final.at[p], zc, along_z, send2.at[p], recv2.at[p])
+
+    def phase2_rest():
+        got(rest_recv.at[0 : (SIDE - 1) * SIDE], rest_sem.at[0])
+        rest_turned[...] = dot(perm[3], rest_recv[...], NN).astype(BF16)
+        spread_out(rest_turned, rest_final, xy, along_xy, rest_send.at[1], rest_sem.at[1])
+
+    def add_rest():
+        got(rest_final.at[0 : (SIDE - 1) * SIDE], rest_sem.at[1])
+        total = jnp.zeros((REST, NVP), F32)
+        for p in range(PAIRS_HERE):
+            total = total + dot(rest_final[...], pk[p], TN)[REST * p : REST * (p + 1)]
+        out[WIDE:NVIR] = (total[:, 0:NVIR] * SCALE).astype(BF16)
 
     def add(p, first=False, last=False):
         got(final.at[p, 0 : (SIDE - 1) * SIDE], recv2.at[p])
-        for a0 in range(0, NVP, 256):
-            rows = pl.ds(a0, 256)
-            term = dot(final[p, :, rows], pk[p], TN)
+        for a0 in range(0, WIDE, 256):
+            n = min(256, WIDE - a0)
+            rows = pl.ds(a0, n)
+            term = dot(final[p, :, rows], pkt[p], TN)
             if not first:
                 term = acc[rows] + term
             if last:
-                n = min(256, NVIR - a0)
-                outb[a0 : a0 + n] = (term[0:n, 0:NVIR] * SCALE).astype(BF16)
-                pltpu.make_async_copy(outb.at[a0 : a0 + n], out.at[a0 : a0 + n], out_sem.at[a0 // 256]).start()
+                out[rows] = (term[:, 0:NVIR] * SCALE).astype(BF16)
             else:
                 acc[rows] = term
 
     phase2(0)
     phase2(1)
     phase2(2)
+    phase2_rest()
     add(0, first=True)
     phase2(3)
+    add_rest()
     add(2)
     add(1)
     add(3, last=True)
@@ -244,24 +290,25 @@
     for p in range(PAIRS_HERE):
         got(half.at[p, 0 : (SIDE - 1) * SIDE], send1.at[p])
         got(turned.at[p, 0 : (SIDE - 1) * SIDE], send2.at[p])
+    got(rest_own.at[0 : (SIDE - 1) * SIDE], rest_send.at[0])
+    got(rest_turned.at[0 : (SIDE - 1) * SIDE], rest_send.at[1])
     got(idx_z.at[0 : SIDE - 1], idx_send.at[0])
     got(idx_all.at[0 : SIDE - 1], idx_send.at[1])
-    for a0 in range(0, NVP, 256):
-        n = min(256, NVIR - a0)
-        pltpu.make_async_copy(outb.at[a0 : a0 + n], out.at[a0 : a0 + n], out_sem.at[a0 // 256]).wait()
 
 
 def shards(ao_slab, screen_mask, pair_ao, occ_coef, vir_coef):
-    any_space = pl.BlockSpec(memory_space=pl.ANY)
-    vmem = pl.BlockSpec(memory_space=pltpu.VMEM)
+    hbm = pl.BlockSpec(memory_space=pltpu.HBM)
+    arrays = (ao_slab, screen_mask.transpose(1, 0, 2), pair_ao.T, occ_coef, vir_coef.T)
     dma = pltpu.SemaphoreType.DMA
     block = pl.pallas_call(
         kernel,
         name="mo_block",
-        out_shape=jax.ShapeDtypeStruct((NVIR, NVIR), BF16),
-        in_specs=[any_space, vmem, vmem, any_space, any_space],
-        out_specs=any_space,
+        out_shape=pltpu.VMEM((NVIR, NVIR), BF16),
+        in_specs=[hbm] * 5,
+        out_specs=pl.BlockSpec(memory_space=pltpu.VMEM),
         scratch_shapes=[
+            pltpu.VMEM((NBLK, PAIRS_HERE, NBLK), jnp.int32),
+            pltpu.VMEM((2, PAIRS_HERE), jnp.int32),
             pltpu.VMEM((PAIRS_HERE, NBF, NBF), BF16),
             pltpu.VMEM((NBP, NOCC), BF16),
             pltpu.VMEM((NVIR, NBF), BF16),
@@ -271,24 +318,30 @@
             pltpu.VMEM((PAIRS_HERE, 32, NBP), F32),
             pltpu.VMEM((NBP, NBP), BF16),
             pltpu.VMEM((NOCC, NBP), BF16),
+            pltpu.VMEM((PAIRS_HERE, NOCC, WIDE), BF16),
+            pltpu.VMEM((PAIRS_HERE, NOCC, WIDE), BF16),
+            pltpu.VMEM((PAIRS_HERE, NOCC, WIDE), BF16),
+            pltpu.VMEM((PAIRS_HERE, NOCC, WIDE), BF16),
+            pltpu.VMEM((PAIRS_HERE, NOCC, 128), BF16),
+            pltpu.VMEM((NOCC, 128), BF16),
+            pltpu.VMEM((NOCC, 128), BF16),
+            pltpu.VMEM((NOCC, 128), BF16),
+            pltpu.VMEM((NOCC, 128), BF16),
             pltpu.VMEM((PAIRS_HERE, NOCC, NVP), BF16),
             pltpu.VMEM((PAIRS_HERE, NOCC, NVP), BF16),
-            pltpu.VMEM((PAIRS_HERE, NOCC, NVP), BF16),
-            pltpu.VMEM((PAIRS_HERE, NOCC, NVP), BF16),
-            pltpu.VMEM((PAIRS_HERE, NOCC, NVP), BF16),
-            pltpu.VMEM((NVP, NVP), F32),
-            pltpu.VMEM((NVIR, NVIR), BF16),
+            pltpu.VMEM((WIDE, NVP), F32),
             pltpu.VMEM((8, 128), jnp.int32),
             pltpu.VMEM((SIDE, 8, 128), jnp.int32),
             pltpu.VMEM((SIDE, 128), jnp.int32),
             pltpu.VMEM((SIDE, SIDE, 128), jnp.int32),
             dma((PAIRS_HERE,)),
+            dma((4,)),
+            dma((PAIRS_HERE,)),
+            dma((PAIRS_HERE,)),
+            dma((PAIRS_HERE,)),
+            dma((PAIRS_HERE,)),
             dma((2,)),
-            dma((4,)),
-            dma((PAIRS_HERE,)),
-            dma((PAIRS_HERE,)),
-            dma((PAIRS_HERE,)),
-            dma((PAIRS_HERE,)),
+            dma((2,)),
             dma((2,)),
             dma((2,)),
         ],
@@ -296,7 +349,7 @@
             collective_id=0, has_side_effects=True, vmem_limit_bytes=56 << 20
         ),
         cost_estimate=pl.CostEstimate(flops=7_000_000_000, bytes_accessed=16_000_000, transcendentals=0),
-    )(ao_slab, screen_mask.transpose(1, 0, 2), pair_ao.T, occ_coef, vir_coef.T)
+    )(*(pltpu.with_memory_space_constraint(x, pltpu.HBM) for x in arrays))
     return block.reshape(1, NVIR, 1, NVIR)
 
 

time: 70.3 us -> 63.3 us (0.900)
  Pallas kernels: 67.3 us -> 62 us
  local copies, waits for them, and re-layouts: 2.89 us -> 1.24 us
    pallas_call x1, Pallas kernels: 67.3 us -> 62 us  [shards(): pl.pallas_call(kernel, name='mo_block', out_shape=pltpu.VMEM((NVIR, NVIR)...]
    unnamed x1, local copies, waits for them, and re-layouts: 2.89 us -> 1.24 us
where the time goes in v2:
time: 63.3 us
  Pallas kernels  62 us (98%)
  local copies, waits for them, and re-layouts  1.24 us (2%)
    pallas_call x1, Pallas kernels, shards(): pl.pallas_call(kernel, name='mo_block', out_shape=pltpu.VMEM((NVIR, NVIR)...  62 us

profile of v2, /device:TPU:1, one launch (start us, length us, event | category | flops | bytes accessed | tf_op | source)
XLA Modules:
  0.0 63.3 jit_solution(3351758856014862965)
XLA Ops:
  0.0 62.0 %mo_block.1 = bf16[900,900]{1,0:T(8,128)(2,1)S(1)} custom-call(bf16[4,1200,1200]{2,1,0:T(8,128)(2,1)} %ao.1, s32[25,4,25]{2,1,0:T(4,128)} %bitcast.6, s32[2,4]{1,0:T(2,128)} %bitcast.7, bf16[1200,256]{1,0:T(8,128)(2,1)} %occ.1, bf16[900,1200]{1,0:T(8,128)(2,1)} %bitcast.5), custom_call_target="tpu_custom_call" | custom-call | flops 7000000000 | bytes 16000000 | tf_op jit(solution)/shard_map/mo_block/pallas_call | solution.py:303
  62.0 1.2 %copy.7 = bf16[1,900,1,900]{3,1,2,0:T(8,128)(2,1)} copy(bf16[1,900,1,900]{3,1,2,0:T(8,128)(2,1)S(1)} %bitcast.4) | data formatting | bytes 3240000

commit v3 on v2

--- a/solution.py
+++ b/solution.py
@@ -20,6 +20,7 @@
 BLK = NBF // NBLK
 PAIRS_HERE = 4
 SIDE = 16
+ORDER = (2, 14, 4, 12, 6, 10, 8, 3, 15, 5, 13, 7, 11, 9, 1)
 PAIRS = 1024
 SCALE = NBF / PAIRS**0.5
 NN = (((1,), (0,)), ((), ()))
@@ -48,37 +49,28 @@
 ):
     grp = lax.axis_index("grp")
     wide = lax.axis_index("wide")
-    zc = lax.rem(grp, SIDE)
-    xy = lax.div(grp, SIDE) * 2 + wide
-
-    def at(xy_of, zc_of):
-        return (lax.div(xy_of, 2) * SIDE + zc_of, lax.rem(xy_of, 2))
-
+    zc = grp & (SIDE - 1)
+    base = grp - zc
+    xy = (grp >> 4) * 2 + wide
+
+    def along_z(to):
+        return (base + to, wide)
+
+    def along_xy(to):
+        return ((to >> 1) * SIDE + zc, to & 1)
+
+    mask_copy = pltpu.make_async_copy(mask, mask_ref, in_sem.at[2])
     occ_copy = pltpu.make_async_copy(occ, occb.at[0:NBF], in_sem.at[0])
     vir_copy = pltpu.make_async_copy(vir, virb, in_sem.at[1])
+    pair_copy = pltpu.make_async_copy(pair, pair_ref, in_sem.at[3])
     ao_copies = [pltpu.make_async_copy(ao.at[p], aob.at[p], ao_sem.at[p]) for p in range(PAIRS_HERE)]
-    mask_copy = pltpu.make_async_copy(mask, mask_ref, in_sem.at[2])
-    pair_copy = pltpu.make_async_copy(pair, pair_ref, in_sem.at[3])
-    mask_copy.start()
-    pair_copy.start()
-    occ_copy.start()
-    ao_copies[0].start()
-    vir_copy.start()
-    for p in range(1, PAIRS_HERE):
-        ao_copies[p].start()
+    for copy in [mask_copy, occ_copy, ao_copies[0], vir_copy, pair_copy] + ao_copies[1:]:
+        copy.start()
 
     barrier = pltpu.get_barrier_semaphore()
-
-    def greet(k, carry):
-        pl.semaphore_signal(
-            barrier, inc=1, device_id=at(xy, lax.rem(zc + k, SIDE)), device_id_type=MESH
-        )
-        pl.semaphore_signal(
-            barrier, inc=1, device_id=at(lax.rem(xy + k, SIDE), zc), device_id_type=MESH
-        )
-        return carry
-
-    lax.fori_loop(1, SIDE, greet, 0)
+    for k in range(1, SIDE):
+        for to in (along_z((zc + k) & (SIDE - 1)), along_xy((xy + k) & (SIDE - 1))):
+            pl.semaphore_signal(barrier, inc=1, device_id=to, device_id_type=MESH)
 
     row = iota((NOCC, NOCC), 0)
     col = iota((NOCC, NOCC), 1)
@@ -88,39 +80,41 @@
     def owner(xy_of, zc_of):
         return (lax.shift_right_logical(xy_of, 1) * SIDE + zc_of) * 2 + (xy_of & 1)
 
-    perm[0] = one_hot(col == owner(lo, hi))
-    perm[1] = one_hot(col == owner(hi, lo))
-    perm[2] = one_hot(col == row)
-    perm[3] = one_hot(col == lo * SIDE + hi)
-
-    block_of = iota((NBLK, NBP), 0) * BLK
-    lane = iota((NBLK, NBP), 1)
-    spread = one_hot((lane >= block_of) & (lane < block_of + BLK))
-    mask_copy.wait()
-    for p in range(PAIRS_HERE):
+    def spread_mask(p):
+        block_of = iota((NBLK, NBP), 0) * BLK
+        lane = iota((NBLK, NBP), 1)
+        spread = one_hot((lane >= block_of) & (lane < block_of + BLK))
         mx[p, 0:NBLK] = dot(mask_ref[:, p, :].astype(F32).astype(BF16), spread, NN)
-
-    lane8 = iota((8, 128), 1)
-    own = jnp.zeros((8, 128), jnp.int32)
-    pair_copy.wait()
-    for p in range(PAIRS_HERE):
-        for q in range(2):
-            own = jnp.where(lane8 == 2 * p + q, pair_ref[q : q + 1, p : p + 1], own)
-    idx_own[...] = own
-    idx_z[zc] = own
 
     scr[NBF:NBP, :] = jnp.zeros((NBP - NBF, NBP), BF16)
     scr[0:NBF, NBP - 128 : NBP] = jnp.zeros((NBF, 128), BF16)
     occb[NBF:NBP, :] = jnp.zeros((NBP - NBF, NOCC), BF16)
     virt[:, NBP - 128 : NBP] = jnp.zeros((NVP, 128), BF16)
-    virt[NVIR - 4 : NVP, :] = jnp.zeros((NVP - NVIR + 4, NBP), BF16)
-
+    virt[WIDE:NVP, :] = jnp.zeros((NVP - WIDE, NBP), BF16)
+    perm[0] = one_hot(col == owner(lo, hi))
+    mask_copy.wait()
+    spread_mask(0)
     occ_copy.wait()
-    for q in range(2):
-        occt[q] = dot(perm[q], occb[...], NT).astype(BF16)
+    occt[0] = dot(perm[0], occb[...], NT).astype(BF16)
+
+    def got(ref, sem):
+        pltpu.make_async_copy(ref, ref, sem).wait()
+
+    def slab(ref, k):
+        return ref.at[pl.ds(pl.multiple_of(k * SIDE, SIDE), SIDE)]
+
+    def spread_out(src, dst, me, to_device, sends, recvs, columns=slice(None)):
+        for k in ORDER:
+            to = (me + k) & (SIDE - 1)
+            pltpu.make_async_remote_copy(
+                src_ref=slab(src, to).at[:, columns], dst_ref=slab(dst, me).at[:, columns],
+                send_sem=sends, recv_sem=recvs,
+                device_id=to_device(to), device_id_type=MESH,
+            ).start()
+        slab(dst, me)[:, columns] = slab(src, me)[:, columns]
 
     def phase1(p, carry):
-        q = lax.rem(p, 2)
+        q = p & 1
         pltpu.make_async_copy(ao.at[0], aob.at[p], ao_sem.at[p]).wait()
 
         def screen(r, c):
@@ -145,58 +139,41 @@
         def _():
             pl.semaphore_wait(barrier, 2 * (SIDE - 1))
 
-            def share(k, c):
+        @pl.when(q == 0)
+        def _():
+            spread_out(half.at[p], recv.at[p], zc, along_z, send1.at[p], recv1.at[p])
+
+        @pl.when(q == 1)
+        def _():
+            spread_out(half.at[p], recv.at[p], xy, along_xy, send1.at[p], recv1.at[p])
+
+        @pl.when(p == 0)
+        def _():
+            pair_copy.wait()
+            lane8 = iota((8, 128), 1)
+            own = jnp.zeros((8, 128), jnp.int32)
+            for pair_here in range(PAIRS_HERE):
+                for j in range(2):
+                    value = pair_ref[j : j + 1, pair_here : pair_here + 1]
+                    own = jnp.where(lane8 == 2 * pair_here + j, value, own)
+            idx_own[...] = own
+            idx_z[zc] = own
+            for k in range(1, SIDE):
                 pltpu.make_async_remote_copy(
                     src_ref=idx_own, dst_ref=idx_z.at[zc],
                     send_sem=idx_send.at[0], recv_sem=idx_recv.at[0],
-                    device_id=at(xy, lax.rem(zc + k, SIDE)), device_id_type=MESH,
+                    device_id=along_z((zc + k) & (SIDE - 1)), device_id_type=MESH,
                 ).start()
-                return c
-
-            lax.fori_loop(1, SIDE, share, 0)
-
-        me = zc + q * (xy - zc)
-
-        def send(k, c):
-            to = lax.rem(me + k, SIDE)
-            pltpu.make_async_remote_copy(
-                src_ref=half.at[p, pl.ds(pl.multiple_of(to * SIDE, SIDE), SIDE)],
-                dst_ref=recv.at[p, pl.ds(pl.multiple_of(me * SIDE, SIDE), SIDE)],
-                send_sem=send1.at[p], recv_sem=recv1.at[p],
-                device_id=at(xy + q * (to - xy), to + q * (zc - to)), device_id_type=MESH,
-            ).start()
-            return c
-
-        lax.fori_loop(1, SIDE, send, 0)
-        mine = pl.ds(pl.multiple_of(me * SIDE, SIDE), SIDE)
-        recv[p, mine] = half[p, mine]
+            perm[1] = one_hot(col == owner(hi, lo))
+            perm[2] = one_hot(col == row)
+            perm[3] = one_hot(col == lo * SIDE + hi)
+            for pair_here in range(1, PAIRS_HERE):
+                spread_mask(pair_here)
+            occt[1] = dot(perm[1], occb[...], NT).astype(BF16)
+
         return carry
 
     lax.fori_loop(0, PAIRS_HERE, phase1, 0)
-
-    def got(ref, sem):
-        pltpu.make_async_copy(ref, ref, sem).wait()
-
-    def slab(ref, k):
-        return ref.at[pl.ds(pl.multiple_of(k * SIDE, SIDE), SIDE)]
-
-    def spread_out(src, dst, me, to_device, sends, recvs):
-        def send(k, c):
-            to = lax.rem(me + k, SIDE)
-            pltpu.make_async_remote_copy(
-                src_ref=slab(src, to), dst_ref=slab(dst, me), send_sem=sends, recv_sem=recvs,
-                device_id=to_device(to), device_id_type=MESH,
-            ).start()
-            return c
-
-        lax.fori_loop(1, SIDE, send, 0)
-        slab(dst, me)[...] = slab(src, me)[...]
-
-    def along_z(to):
-        return at(xy, to)
-
-    def along_xy(to):
-        return at(to, zc)
 
     shift_row = iota((128, 128), 0)
     shift_col = iota((128, 128), 1)
@@ -213,16 +190,12 @@
     idx_zrow[...] = idx_z[:, 0, :]
     idx_all[xy] = idx_z[:, 0, :]
 
-    def share2(k, c):
+    for k in range(1, SIDE):
         pltpu.make_async_remote_copy(
             src_ref=idx_zrow, dst_ref=idx_all.at[xy],
             send_sem=idx_send.at[1], recv_sem=idx_recv.at[1],
-            device_id=at(lax.rem(xy + k, SIDE), zc), device_id_type=MESH,
+            device_id=along_xy((xy + k) & (SIDE - 1)), device_id_type=MESH,
         ).start()
-        return c
-
-    lax.fori_loop(1, SIDE, share2, 0)
-    got(idx_all.at[0 : SIDE - 1], idx_recv.at[1])
 
     lane_all = iota((NOCC, 128), 1)
     basis = iota((NOCC, NBP), 1)
@@ -237,19 +210,19 @@
         rows = dot(one_hot(basis == chosen(2 * p + 1)), virt[...], NT)
         kernel_rows = (lam * rows).astype(BF16)
         pk[p] = kernel_rows
-        pkt[p] = dot(perm[2 + lax.rem(p, 2)], kernel_rows, NN).astype(BF16)
+        pkt[p] = dot(perm[2 + (p & 1)], kernel_rows, NN).astype(BF16)
         return c
 
-    lax.fori_loop(0, PAIRS_HERE, build, 0)
 
     def phase2(p):
-        q = p % 2
         got(recv.at[p, 0 : (SIDE - 1) * SIDE], recv1.at[p])
         turned[p] = dot(perm[3], recv[p], NN).astype(BF16)
-        if q == 0:
-            spread_out(turned.at[p], final.at[p], xy, along_xy, send2.at[p], recv2.at[p])
-        else:
-            spread_out(turned.at[p], final.at[p], zc, along_z, send2.at[p], recv2.at[p])
+        me, to_device = (zc, along_z) if p % 2 else (xy, along_xy)
+        for part, columns in enumerate(parts_of(p)):
+            spread_out(turned.at[p], final.at[p], me, to_device, send2.at[p], recv2.at[p, part], columns)
+
+    def parts_of(p):
+        return (slice(0, WIDE),)
 
     def phase2_rest():
         got(rest_recv.at[0 : (SIDE - 1) * SIDE], rest_sem.at[0])
@@ -264,26 +237,28 @@
         out[WIDE:NVIR] = (total[:, 0:NVIR] * SCALE).astype(BF16)
 
     def add(p, first=False, last=False):
-        got(final.at[p, 0 : (SIDE - 1) * SIDE], recv2.at[p])
-        for a0 in range(0, WIDE, 256):
-            n = min(256, WIDE - a0)
-            rows = pl.ds(a0, n)
-            term = dot(final[p, :, rows], pkt[p], TN)
-            if not first:
-                term = acc[rows] + term
-            if last:
-                out[rows] = (term[:, 0:NVIR] * SCALE).astype(BF16)
-            else:
-                acc[rows] = term
+        for part, columns in enumerate(parts_of(p)):
+            got(final.at[p, 0 : (SIDE - 1) * SIDE, columns], recv2.at[p, part])
+            for a0 in range(columns.start, columns.stop, 256):
+                rows = pl.ds(a0, min(256, WIDE - a0))
+                term = dot(final[p, :, rows], pkt[p], TN)
+                if not first:
+                    term = acc[rows] + term
+                if last:
+                    out[rows] = (term[:, 0:NVIR] * SCALE).astype(BF16)
+                else:
+                    acc[rows] = term
 
     phase2(0)
     phase2(1)
+    got(idx_all.at[0 : SIDE - 1], idx_recv.at[1])
+    lax.fori_loop(0, PAIRS_HERE, build, 0)
     phase2(2)
+    phase2(3)
     phase2_rest()
     add(0, first=True)
-    phase2(3)
+    add(2)
     add_rest()
-    add(2)
     add(1)
     add(3, last=True)
 
@@ -339,7 +314,7 @@
             dma((PAIRS_HERE,)),
             dma((PAIRS_HERE,)),
             dma((PAIRS_HERE,)),
-            dma((PAIRS_HERE,)),
+            dma((PAIRS_HERE, 2)),
             dma((2,)),
             dma((2,)),
             dma((2,)),

time: 63.3 us -> 58.6 us (0.926)
  Pallas kernels: 62 us -> 57.3 us
    pallas_call x1, Pallas kernels: 62 us -> 57.3 us  [shards(): pl.pallas_call(kernel, name='mo_block', out_shape=pltpu.VMEM((NVIR, NVIR)...]
where the time goes in v3:
time: 58.6 us
  Pallas kernels  57.3 us (98%)
  local copies, waits for them, and re-layouts  1.24 us (2%)
    pallas_call x1, Pallas kernels, shards(): pl.pallas_call(kernel, name='mo_block', out_shape=pltpu.VMEM((NVIR, NVIR)...  57.3 us
    unnamed x1, local copies, waits for them, and re-layouts  1.24 us

profile of v3, /device:TPU:1, one launch (start us, length us, event | category | flops | bytes accessed | tf_op | source)
XLA Modules:
  0.0 58.6 jit_solution(11674439967491962446)
XLA Ops:
  0.0 57.3 %mo_block.1 = bf16[900,900]{1,0:T(8,128)(2,1)S(1)} custom-call(bf16[4,1200,1200]{2,1,0:T(8,128)(2,1)} %ao.1, s32[25,4,25]{2,1,0:T(4,128)} %bitcast.6, s32[2,4]{1,0:T(2,128)} %bitcast.7, bf16[1200,256]{1,0:T(8,128)(2,1)} %occ.1, bf16[900,1200]{1,0:T(8,128)(2,1)} %bitcast.5), custom_call_target="tpu_custom_call" | custom-call | flops 7000000000 | bytes 16000000 | tf_op jit(solution)/shard_map/mo_block/pallas_call | solution.py:278
  57.3 1.2 %copy.7 = bf16[1,900,1,900]{3,1,2,0:T(8,128)(2,1)} copy(bf16[1,900,1,900]{3,1,2,0:T(8,128)(2,1)S(1)} %bitcast.4) | data formatting | bytes 3240000

commit v4 on v3

--- a/solution.py
+++ b/solution.py
@@ -43,7 +43,7 @@
 def kernel(
     ao, mask, pair, occ, vir, out,
     mask_ref, pair_ref, aob, occb, virb, virt, occt, perm, mx, scr, left, half, recv, turned, final,
-    rest, rest_own, rest_recv, rest_turned, rest_final, pk, pkt, acc,
+    rest, rest_own, rest_z, rest_turned, rest_final, pk, pkt, acc,
     idx_own, idx_z, idx_zrow, idx_all,
     ao_sem, in_sem, send1, recv1, send2, recv2, rest_send, rest_sem, idx_send, idx_recv,
 ):
@@ -150,12 +150,12 @@
         @pl.when(p == 0)
         def _():
             pair_copy.wait()
-            lane8 = iota((8, 128), 1)
-            own = jnp.zeros((8, 128), jnp.int32)
+            lane_own = iota((1, 128), 1)
+            own = jnp.zeros((1, 128), jnp.int32)
             for pair_here in range(PAIRS_HERE):
                 for j in range(2):
                     value = pair_ref[j : j + 1, pair_here : pair_here + 1]
-                    own = jnp.where(lane8 == 2 * pair_here + j, value, own)
+                    own = jnp.where(lane_own == 2 * pair_here + j, value, own)
             idx_own[...] = own
             idx_z[zc] = own
             for k in range(1, SIDE):
@@ -175,16 +175,31 @@
 
     lax.fori_loop(0, PAIRS_HERE, phase1, 0)
 
-    shift_row = iota((128, 128), 0)
-    shift_col = iota((128, 128), 1)
+    lane_row = iota((128, 128), 0)
+    lane_col = iota((128, 128), 1)
     total = jnp.zeros((NOCC, 128), F32)
     for p in range(PAIRS_HERE):
-        moved = dot(rest[p], one_hot((shift_col == shift_row + REST * p) & (shift_row < REST)), NN)
+        moved = dot(rest[p], one_hot(((lane_col & 15) == lane_row + REST * p) & (lane_row < REST)), NN)
         if p % 2:
             moved = dot(perm[3], moved.astype(BF16), NN)
         total = total + moved
-    rest_own[...] = total.astype(BF16)
-    spread_out(rest_own, rest_recv, zc, along_z, rest_send.at[0], rest_sem.at[0])
+    rest_row = iota((NOCC, 128), 0)
+    in_group = lax.shift_right_logical(iota((NOCC, 128), 1), 4) == (rest_row & 7)
+    low_half = (rest_row & 8) == 0
+    picked = jnp.where(in_group, total, 0.0).astype(BF16)
+    fold_row = iota((SIDE, NOCC), 0)
+    fold_col = iota((SIDE, NOCC), 1)
+    for h in range(2):
+        fold = (lax.shift_right_logical(fold_col, 4) == fold_row) & ((fold_col & 8) == 8 * h)
+        rest_own[:, h, :] = dot(one_hot(fold), picked, NN)
+    rest_z[zc] = rest_own[zc]
+    for k in ORDER:
+        to = (zc + k) & (SIDE - 1)
+        pltpu.make_async_remote_copy(
+            src_ref=rest_own.at[to], dst_ref=rest_z.at[zc],
+            send_sem=rest_send.at[0], recv_sem=rest_sem.at[0],
+            device_id=along_z(to), device_id_type=MESH,
+        ).start()
 
     got(idx_z.at[0 : SIDE - 1], idx_recv.at[0])
     idx_zrow[...] = idx_z[:, 0, :]
@@ -222,11 +237,16 @@
             spread_out(turned.at[p], final.at[p], me, to_device, send2.at[p], recv2.at[p, part], columns)
 
     def parts_of(p):
-        return (slice(0, WIDE),)
+        return (slice(0, 512), slice(512, WIDE)) if p == PAIRS_HERE - 1 else (slice(0, WIDE),)
 
     def phase2_rest():
-        got(rest_recv.at[0 : (SIDE - 1) * SIDE], rest_sem.at[0])
-        rest_turned[...] = dot(perm[3], rest_recv[...], NN).astype(BF16)
+        got(rest_z.at[0 : SIDE - 1], rest_sem.at[0])
+        source = one_hot(lax.shift_right_logical(iota((NOCC, SIDE), 0), 4) == iota((NOCC, SIDE), 1))
+        halves = [dot(source, rest_z[:, h, :].astype(BF16), NN) for h in range(2)]
+        unfolded = jnp.where(in_group, jnp.where(low_half, halves[0], halves[1]), 0.0).astype(BF16)
+        unfold = one_hot(((lane_row & 15) == lane_col) & (lane_col < SIDE))
+        received = dot(unfolded, unfold, NN).astype(BF16)
+        rest_turned[...] = dot(perm[3], received, NN).astype(BF16)
         spread_out(rest_turned, rest_final, xy, along_xy, rest_send.at[1], rest_sem.at[1])
 
     def add_rest():
@@ -251,11 +271,11 @@
 
     phase2(0)
     phase2(1)
-    got(idx_all.at[0 : SIDE - 1], idx_recv.at[1])
-    lax.fori_loop(0, PAIRS_HERE, build, 0)
     phase2(2)
     phase2(3)
     phase2_rest()
+    got(idx_all.at[0 : SIDE - 1], idx_recv.at[1])
+    lax.fori_loop(0, PAIRS_HERE, build, 0)
     add(0, first=True)
     add(2)
     add_rest()
@@ -265,7 +285,7 @@
     for p in range(PAIRS_HERE):
         got(half.at[p, 0 : (SIDE - 1) * SIDE], send1.at[p])
         got(turned.at[p, 0 : (SIDE - 1) * SIDE], send2.at[p])
-    got(rest_own.at[0 : (SIDE - 1) * SIDE], rest_send.at[0])
+    got(rest_own.at[0 : SIDE - 1], rest_send.at[0])
     got(rest_turned.at[0 : (SIDE - 1) * SIDE], rest_send.at[1])
     got(idx_z.at[0 : SIDE - 1], idx_send.at[0])
     got(idx_all.at[0 : SIDE - 1], idx_send.at[1])
@@ -298,15 +318,15 @@
             pltpu.VMEM((PAIRS_HERE, NOCC, WIDE), BF16),
             pltpu.VMEM((PAIRS_HERE, NOCC, WIDE), BF16),
             pltpu.VMEM((PAIRS_HERE, NOCC, 128), BF16),
-            pltpu.VMEM((NOCC, 128), BF16),
-            pltpu.VMEM((NOCC, 128), BF16),
+            pltpu.VMEM((SIDE, 2, 128), F32),
+            pltpu.VMEM((SIDE, 2, 128), F32),
             pltpu.VMEM((NOCC, 128), BF16),
             pltpu.VMEM((NOCC, 128), BF16),
             pltpu.VMEM((PAIRS_HERE, NOCC, NVP), BF16),
             pltpu.VMEM((PAIRS_HERE, NOCC, NVP), BF16),
             pltpu.VMEM((WIDE, NVP), F32),
-            pltpu.VMEM((8, 128), jnp.int32),
-            pltpu.VMEM((SIDE, 8, 128), jnp.int32),
+            pltpu.VMEM((1, 128), jnp.int32),
+            pltpu.VMEM((SIDE, 1, 128), jnp.int32),
             pltpu.VMEM((SIDE, 128), jnp.int32),
             pltpu.VMEM((SIDE, SIDE, 128), jnp.int32),
             dma((PAIRS_HERE,)),

time: 58.6 us -> 56.1 us (0.957)
  Pallas kernels: 57.3 us -> 54.7 us
    pallas_call x1, Pallas kernels: 57.3 us -> 54.7 us  [shards(): pl.pallas_call(kernel, name='mo_block', out_shape=pltpu.VMEM((NVIR, NVIR)...]
where the time goes in v4:
time: 56.1 us; the launch traced here: 56 us
  Pallas kernels  54.7 us (98%)
  local copies, waits for them, and re-layouts  1.24 us (2%)
    pallas_call x1, Pallas kernels, shards(): pl.pallas_call(kernel, name='mo_block', out_shape=pltpu.VMEM((NVIR, NVIR)...  54.7 us
    unnamed x1, local copies, waits for them, and re-layouts  1.24 us

profile of v4, /device:TPU:1, one launch (start us, length us, event | category | flops | bytes accessed | tf_op | source)
XLA Modules:
  0.0 56.0 jit_solution(5889191951776101654)
XLA Ops:
  0.0 54.7 %mo_block.1 = bf16[900,900]{1,0:T(8,128)(2,1)S(1)} custom-call(bf16[4,1200,1200]{2,1,0:T(8,128)(2,1)} %ao.1, s32[25,4,25]{2,1,0:T(4,128)} %bitcast.6, s32[2,4]{1,0:T(2,128)} %bitcast.7, bf16[1200,256]{1,0:T(8,128)(2,1)} %occ.1, bf16[900,1200]{1,0:T(8,128)(2,1)} %bitcast.5), custom_call_target="tpu_custom_call" | custom-call | flops 7000000000 | bytes 16000000 | tf_op jit(solution)/shard_map/mo_block/pallas_call | solution.py:298
  54.7 1.2 %copy.7 = bf16[1,900,1,900]{3,1,2,0:T(8,128)(2,1)} copy(bf16[1,900,1,900]{3,1,2,0:T(8,128)(2,1)S(1)} %bitcast.4) | data formatting | bytes 3240000

commit v5 on v4

--- a/solution.py
+++ b/solution.py
@@ -20,7 +20,7 @@
 BLK = NBF // NBLK
 PAIRS_HERE = 4
 SIDE = 16
-ORDER = (2, 14, 4, 12, 6, 10, 8, 3, 15, 5, 13, 7, 11, 9, 1)
+ORDER = (8, 9, 6, 10, 7, 11, 4, 12, 5, 13, 2, 14, 3, 15, 1)
 PAIRS = 1024
 SCALE = NBF / PAIRS**0.5
 NN = (((1,), (0,)), ((), ()))
@@ -63,8 +63,11 @@
     occ_copy = pltpu.make_async_copy(occ, occb.at[0:NBF], in_sem.at[0])
     vir_copy = pltpu.make_async_copy(vir, virb, in_sem.at[1])
     pair_copy = pltpu.make_async_copy(pair, pair_ref, in_sem.at[3])
-    ao_copies = [pltpu.make_async_copy(ao.at[p], aob.at[p], ao_sem.at[p]) for p in range(PAIRS_HERE)]
-    for copy in [mask_copy, occ_copy, ao_copies[0], vir_copy, pair_copy] + ao_copies[1:]:
+
+    def ao_copy(p):
+        return pltpu.make_async_copy(ao.at[p], aob.at[p], ao_sem.at[p])
+
+    for copy in (mask_copy, occ_copy, ao_copy(0), vir_copy, pair_copy):
         copy.start()
 
     barrier = pltpu.get_barrier_semaphore()
@@ -115,7 +118,12 @@
 
     def phase1(p, carry):
         q = p & 1
-        pltpu.make_async_copy(ao.at[0], aob.at[p], ao_sem.at[p]).wait()
+        ao_copy(p).wait()
+
+        @pl.when(p < PAIRS_HERE - 1)
+        def _():
+            ao_copy(p + 1).start()
+
 
         def screen(r, c):
             rows = pl.ds(pl.multiple_of(r * BLK, BLK), BLK)

time: 56.1 us -> 54.8 us (0.977)
  Pallas kernels: 54.7 us -> 53.5 us
    pallas_call x1, Pallas kernels: 54.7 us -> 53.5 us  [shards(): pl.pallas_call(kernel, name='mo_block', out_shape=pltpu.VMEM((NVIR, NVIR)...]
where the time goes in v5:
time: 54.8 us; the launch traced here: 54.7 us
  Pallas kernels  53.5 us (98%)
  local copies, waits for them, and re-layouts  1.24 us (2%)
    pallas_call x1, Pallas kernels, shards(): pl.pallas_call(kernel, name='mo_block', out_shape=pltpu.VMEM((NVIR, NVIR)...  53.5 us
    unnamed x1, local copies, waits for them, and re-layouts  1.24 us

profile of v5, /device:TPU:1, one launch (start us, length us, event | category | flops | bytes accessed | tf_op | source)
XLA Modules:
  0.0 54.7 jit_solution(11180533650929917577)
XLA Ops:
  0.0 53.5 %mo_block.1 = bf16[900,900]{1,0:T(8,128)(2,1)S(1)} custom-call(bf16[4,1200,1200]{2,1,0:T(8,128)(2,1)} %ao.1, s32[25,4,25]{2,1,0:T(4,128)} %bitcast.6, s32[2,4]{1,0:T(2,128)} %bitcast.7, bf16[1200,256]{1,0:T(8,128)(2,1)} %occ.1, bf16[900,1200]{1,0:T(8,128)(2,1)} %bitcast.5), custom_call_target="tpu_custom_call" | custom-call | flops 7000000000 | bytes 16000000 | tf_op jit(solution)/shard_map/mo_block/pallas_call | solution.py:306
  53.5 1.2 %copy.7 = bf16[1,900,1,900]{3,1,2,0:T(8,128)(2,1)} copy(bf16[1,900,1,900]{3,1,2,0:T(8,128)(2,1)S(1)} %bitcast.4) | data formatting | bytes 3240000

commit v6 on v5

--- a/solution.py
+++ b/solution.py
@@ -139,9 +139,7 @@
             vir_copy.wait()
             virt[0:NVIR, 0:NBF] = virb[...]
 
-        both = dot(left[...], virt[...], NT)
-        half[p] = both[:, 0:WIDE].astype(BF16)
-        rest[p] = both[:, WIDE:NVP].astype(BF16)
+        half[p, :, 0:512] = dot(left[...], virt[0:512], NT).astype(BF16)
 
         @pl.when(p == 0)
         def _():
@@ -149,7 +147,15 @@
 
         @pl.when(q == 0)
         def _():
-            spread_out(half.at[p], recv.at[p], zc, along_z, send1.at[p], recv1.at[p])
+            spread_out(half.at[p], recv.at[p], zc, along_z, send1.at[p], recv1.at[p], slice(0, 512))
+
+        both = dot(left[...], virt[512:NVP], NT)
+        half[p, :, 512:WIDE] = both[:, 0 : WIDE - 512].astype(BF16)
+        rest[p] = both[:, WIDE - 512 : NVP - 512].astype(BF16)
+
+        @pl.when(q == 0)
+        def _():
+            spread_out(half.at[p], recv.at[p], zc, along_z, send1.at[p], recv1.at[p], slice(512, WIDE))
 
         @pl.when(q == 1)
         def _():

time: 54.8 us -> 54.8 us (level)
  no operation moved by 1% of the time
where the time goes in v6:
time: 54.8 us; the launch traced here: 54.7 us
  Pallas kernels  53.5 us (98%)
  local copies, waits for them, and re-layouts  1.24 us (2%)
    pallas_call x1, Pallas kernels, shards(): pl.pallas_call(kernel, name='mo_block', out_shape=pltpu.VMEM((NVIR, NVIR)...  53.5 us
    unnamed x1, local copies, waits for them, and re-layouts  1.24 us

profile of v6, /device:TPU:1, one launch (start us, length us, event | category | flops | bytes accessed | tf_op | source)
XLA Modules:
  0.0 54.7 jit_solution(925630724489120570)
XLA Ops:
  0.0 53.5 %mo_block.1 = bf16[900,900]{1,0:T(8,128)(2,1)S(1)} custom-call(bf16[4,1200,1200]{2,1,0:T(8,128)(2,1)} %ao.1, s32[25,4,25]{2,1,0:T(4,128)} %bitcast.6, s32[2,4]{1,0:T(2,128)} %bitcast.7, bf16[1200,256]{1,0:T(8,128)(2,1)} %occ.1, bf16[900,1200]{1,0:T(8,128)(2,1)} %bitcast.5), custom_call_target="tpu_custom_call" | custom-call | flops 7000000000 | bytes 16000000 | tf_op jit(solution)/shard_map/mo_block/pallas_call | solution.py:312
  53.5 1.2 %copy.7 = bf16[1,900,1,900]{3,1,2,0:T(8,128)(2,1)} copy(bf16[1,900,1,900]{3,1,2,0:T(8,128)(2,1)S(1)} %bitcast.4) | data formatting | bytes 3240000
